TPU v7x, 32 devices: a whole 2x2x4 slice. The times are simulated.
32 devices in a mesh: blk: 4 (over z), grp: 8 (over y, x, core).
Axes of the slice: x: 2, y: 2, z: 4, core: 2. Of those that a mesh axis runs over, the one named last changes fastest.
Arguments:
- picture_embeddings_raw: bfloat16 [4096, 1152], P(('blk', 'grp')), may hold values from -6 to 6
- caption_feature_input: bfloat16 [4096, 1152], P(('blk', 'grp')), may hold values from -0.29882812 to 0.29882812
- caption_mapping_weights: bfloat16 [1152, 1152], replicated, may hold values from -0.1875 to 0.1875
- sharpness_array: float32 [1], replicated, may hold values from 10 to 40
- affinity_shift: float32 [1], replicated, may hold values from -4 to -1
Outputs:
- text_grad: bfloat16 [4096, 1152], P(('blk', 'grp'))
- head_grad: float32 [1152, 1152], P('grp', 'blk')
All inputs are finite; a program needn't handle non-finite values.
Results may differ from a plain program's by a relative error of at most 0.017.
Values may be sent and summed in bfloat16 or wider, within the bound.
A program may use at most 64 MiB of HBM per device.

v0:
```python
import jax
import jax.numpy as jnp
from jax import lax
from jax.sharding import PartitionSpec as P


def shifted(block, axis, distance):
    devices = range(lax.axis_size(axis))
    route = [((i - distance) % len(devices), i) for i in devices]
    return lax.ppermute(block, axis, route)


def unit_rows(values):
    radius = jnp.sqrt(jnp.sum(values * values, axis=1, keepdims=True) + 1e-06)
    return (values / radius, radius)


def pair_grad(images, texts, labels, sharpness_factor, neighbour_distance):
    pair_scores = (
        sharpness_factor * jnp.dot(images, texts.T, preferred_element_type=jnp.float32)
        + neighbour_distance
    )
    weights = (jax.nn.sigmoid(pair_scores) - labels).astype(jnp.bfloat16)
    return sharpness_factor * lax.dot_general(
        weights, images, (((0,), (0,)), ((), ())), preferred_element_type=jnp.float32
    )


def local(
    picture_embeddings_raw,
    caption_feature_input,
    caption_mapping_weights,
    sharpness_array,
    affinity_shift,
):
    sharpness_factor = sharpness_array[0]
    neighbour_distance = affinity_shift[0]
    rows_here = picture_embeddings_raw.shape[0]
    image_unit = unit_rows(picture_embeddings_raw.astype(jnp.float32))[0].astype(jnp.bfloat16)
    projected = jnp.dot(
        caption_feature_input, caption_mapping_weights, preferred_element_type=jnp.float32
    )
    unit, radius = unit_rows(projected)
    text_unit = unit.astype(jnp.bfloat16)
    labels = jnp.eye(rows_here, dtype=jnp.float32)
    local_segment = pair_grad(image_unit, text_unit, labels, sharpness_factor, neighbour_distance)
    earlier = shifted(text_unit, "blk", 1)
    remote_part = pair_grad(image_unit, earlier, 0.0, sharpness_factor, neighbour_distance)
    returned = shifted(remote_part.astype(jnp.bfloat16), "blk", -1).astype(remote_part.dtype)
    unit_grad = local_segment + returned
    row_grad = (
        (unit_grad - unit * jnp.sum(unit * unit_grad, axis=1, keepdims=True)) / radius
    ).astype(jnp.bfloat16)
    text_grad = lax.dot_general(
        row_grad,
        caption_mapping_weights,
        (((1,), (1,)), ((), ())),
        preferred_element_type=jnp.float32,
    ).astype(jnp.bfloat16)
    incomplete_sum = lax.psum_scatter(
        lax.dot_general(
            caption_feature_input,
            row_grad,
            (((0,), (0,)), ((), ())),
            preferred_element_type=jnp.float32,
        ).astype(jnp.bfloat16),
        "grp",
        scatter_dimension=0,
        tiled=True,
    )
    head_grad = lax.psum_scatter(incomplete_sum, "blk", scatter_dimension=1, tiled=True).astype(
        jnp.float32
    )
    return (text_grad, head_grad)


def solution(mesh):
    return jax.shard_map(
        local,
        mesh=mesh,
        in_specs=(P(("blk", "grp"), None), P(("blk", "grp"), None), P(), P(), P()),
        out_specs=(P(("blk", "grp"), None), P("grp", "blk")),
        check_vma=False,
    )
```

profile of v0, /device:TPU:0, one launch (start us, length us, event | category | flops | bytes accessed | tf_op | source)
XLA Modules:
  0.0 123.6 jit_solution(13545835632849622662)
XLA Ops:
  7.2 0.0 copy-start
  7.2 0.0 copy-start.1
  7.2 0.0 reduce-scatter.7.cloned.1.call-start
  7.2 1.7 %copy-done = bf16[1152,1152]{1,0:T(8,128)(2,1)S(1)} copy-done((bf16[1152,1152]{1,0:T(8,128)(2,1)S(1)}, bf16[1152,1152]{1,0:T(8,128)(2,1)}, u32[]{:S(2)}) %copy-start) | copy-done | bytes 2654232
  8.9 1.7 %multiply_reduce_fusion.1 = (f32[128]{0:T(128)S(1)}, f32[128,1152]{1,0:T(8,128)S(1)}) fusion(bf16[128,1152]{1,0:T(8,128)(2,1)} %param.6, bf16[1152,1152]{1,0:T(8,128)(2,1)S(1)} %copy-done), kind=kOutput, calls=%fused_computation.28 | convolution fusion | flops 340033408 | bytes 3539456 | tf_op jit(solution)/shard_map/dot_general | solution.py:40
  10.6 0.1 fusion.30
  10.7 3.1 %collective-permute-start = (bf16[128,1152]{1,0:T(8,128)(2,1)S(1)}, bf16[128,1152]{1,0:T(8,128)(2,1)S(1)}, u32[]{:S(2)}, u32[]{:S(2)}) collective-permute-start(bf16[128,1152]{1,0:T(8,128)(2,1)S(1)} %fusion.30), channel_id=1, source_target_pairs={{24,0},{0,8},{8,16},{16,24},{25,1},{1,9},{9,17},{17,25},{26,2},{2,... | collective-permute-start | bytes 884744 | tf_op jit(solution)/shard_map/ppermute | solution.py:10
  15.1 0.0 copy-done.1
  15.1 0.1 fusion.15
  15.3 7.6 %collective-permute-done = bf16[128,1152]{1,0:T(8,128)(2,1)S(1)} collective-permute-done((bf16[128,1152]{1,0:T(8,128)(2,1)S(1)}, bf16[128,1152]{1,0:T(8,128)(2,1)S(1)}, u32[]{:S(2)}, u32[]{:S(2)}) %collective-permute-start) | collective-permute-done | bytes 294944 | tf_op jit(solution)/shard_map/ppermute | solution.py:10
  22.8 0.0 copy-start.2
  22.8 0.7 copy-done.2
  23.5 2.3 %fusion.1 = bf16[128,1152]{1,0:T(8,128)(2,1)} fusion(bf16[128,1152]{1,0:T(8,128)(2,1)} %copy-done.2, f32[]{:T(128)} %bitcast.11, f32[]{:T(128)} %bitcast.13, bf16[128,1152]{1,0:T(8,128)(2,1)S(1)} %copy-done.1, f32[128]{0:T(128)S(1)} %add_sqrt_fusion.1), kind=kOutput, calls=%fused_computation.4 | convolution fusion | flops 76775424 | bytes 885256 | tf_op jit(solution)/shard_map/dot_general | solution.py:24
  25.9 1.7 %collective-permute-start.1 = (bf16[128,1152]{1,0:T(8,128)(2,1)}, bf16[128,1152]{1,0:T(8,128)(2,1)}, u32[]{:S(2)}, u32[]{:S(2)}) collective-permute-start(bf16[128,1152]{1,0:T(8,128)(2,1)} %fusion.1), channel_id=1, source_target_pairs={{8,0},{16,8},{24,16},{0,24},{9,1},{17,9},{25,17},{1,25},{10,2},{18... | collective-permute-start | bytes 884744 | tf_op jit(solution)/shard_map/ppermute | solution.py:10
  27.6 6.8 %collective-permute-done.1 = bf16[128,1152]{1,0:T(8,128)(2,1)} collective-permute-done((bf16[128,1152]{1,0:T(8,128)(2,1)}, bf16[128,1152]{1,0:T(8,128)(2,1)}, u32[]{:S(2)}, u32[]{:S(2)}) %collective-permute-start.1) | collective-permute-done | bytes 294944 | tf_op jit(solution)/shard_map/ppermute | solution.py:10
  34.4 2.5 %multiply_reduce_fusion = (f32[128]{0:T(128)S(1)}, f32[128,1152]{1,0:T(8,128)}) fusion(bf16[128,1152]{1,0:T(8,128)(2,1)} %collective-permute-done.1, f32[128,1152]{1,0:T(8,128)S(1)} %get-tuple-element.7, f32[128]{0:T(128)S(1)} %add_sqrt_fusion, bf16[128,1152]{1,0:T(8,128)(2,1)S(1)} %copy-done.1, f32[128]{0:T(128)S(1)} %add_sqrt_fusion.1, f32[]{:T(128)} %bitcast.12, ...), kind=kOutput, calls=%fused_computation.26 | convolution fusion | flops 77709184 | bytes 1771016 | tf_op jit(solution)/shard_map/dot_general | solution.py:24
  36.9 3.7 %fusion = bf16[1152,1152]{0,1:T(8,128)(2,1)} fusion(bf16[128,1152]{1,0:T(8,128)(2,1)} %param.6, f32[128,1152]{1,0:T(8,128)} %get-tuple-element.9, bf16[128,1152]{1,0:T(8,128)(2,1)} %collective-permute-done.1, f32[128]{0:T(128)S(1)} %get-tuple-element.8, f32[128]{0:T(128)S(1)} %add_sqrt_fusion, f32[128,1152]{1,0:T(8,128)S(1)} %get-tuple-element.7), kind=kOutput, calls=%fused_computation.1 | convolution fusion | flops 342097920 | bytes 4424704 | tf_op jit(solution)/shard_map/dot_general | solution.py:61
  40.6 5.2 %copy.9 = bf16[1152,1152]{1,0:T(8,128)(2,1)} copy(bf16[1152,1152]{0,1:T(8,128)(2,1)} %fusion) | data formatting | bytes 5308416
  45.8 0.0 reduce-scatter.7.cloned.1.call-update
  45.8 0.0 reduce-scatter.5.cloned.1.call-start
  45.9 44.7 %reduce-scatter.7.cloned.1.call-done = bf16[144,1152]{1,0:T(8,128)(2,1)} async-done(((bf16[1152,1152]{1,0:T(8,128)(2,1)}), bf16[144,1152]{1,0:T(8,128)(2,1)}) %reduce-scatter.7.cloned.1.call-update) | async-done | bytes 331792
  90.6 2.0 %copy.10 = bf16[144,1152]{0,1:T(8,128)(2,1)} copy(bf16[144,1152]{1,0:T(8,128)(2,1)} %reduce-scatter.7.cloned.1.call-done) | data formatting | bytes 663552
  92.6 0.0 reduce-scatter.5.cloned.1.call-update
  92.7 2.8 %convolution_convert_fusion.1 = bf16[128,1152]{1,0:T(8,128)(2,1)} fusion(bf16[1152,1152]{1,0:T(8,128)(2,1)S(1)} %copy-done, f32[128,1152]{1,0:T(8,128)} %get-tuple-element.9, bf16[128,1152]{1,0:T(8,128)(2,1)} %collective-permute-done.1, f32[128]{0:T(128)S(1)} %get-tuple-element.8, f32[128]{0:T(128)S(1)} %add_sqrt_fusion, f32[128,1152]{1,0:T(8,128)S(1)} %get-tuple-element.7), kind=kOutput, calls=%fused_computation.5 | convolution fusion | flops 340918272 | bytes 4424704 | tf_op jit(solution)/shard_map/dot_general | solution.py:54
  95.5 19.6 %reduce-scatter.5.cloned.1.call-done = bf16[144,288]{0,1:T(8,128)(2,1)} async-done(((bf16[144,1152]{0,1:T(8,128)(2,1)}), bf16[144,288]{0,1:T(8,128)(2,1)}) %reduce-scatter.5.cloned.1.call-update) | async-done | bytes 82960 | tf_op jit(solution)/shard_map/reduce_scatter | solution.py:71
  115.0 1.7 %copy.8 = f32[144,288]{1,0:T(8,128)} copy(bf16[144,288]{0,1:T(8,128)(2,1)} %reduce-scatter.5.cloned.1.call-done) | data formatting | bytes 248832
  (2 shorter events, 0.0 us)
Async XLA Ops:
  7.2 1.8 %copy-start = (bf16[1152,1152]{1,0:T(8,128)(2,1)S(1)}, bf16[1152,1152]{1,0:T(8,128)(2,1)}, u32[]{:S(2)}) copy-start(bf16[1152,1152]{1,0:T(8,128)(2,1)} %param.7) | copy-start | bytes 7962628
  7.2 7.9 %copy-start.1 = (bf16[128,1152]{1,0:T(8,128)(2,1)S(1)}, bf16[128,1152]{1,0:T(8,128)(2,1)}, u32[]{:S(2)}) copy-start(bf16[128,1152]{1,0:T(8,128)(2,1)} %param.5) | copy-start | bytes 884740
  7.2 83.4 %reduce-scatter.7.cloned.1.call-start = ((), (), s32[]{:S(2)}) async-start(), calls=%async_computation.3 | async-start | bytes 2985984
  10.7 12.1 %collective-permute-start = (bf16[128,1152]{1,0:T(8,128)(2,1)S(1)}, bf16[128,1152]{1,0:T(8,128)(2,1)S(1)}, u32[]{:S(2)}, u32[]{:S(2)}) collective-permute-start(bf16[128,1152]{1,0:T(8,128)(2,1)S(1)} %fusion.30), channel_id=1, source_target_pairs={{24,0},{0,8},{8,16},{16,24},{25,1},{1,9},{9,17},{17,25},{26,2},{2,... | collective-permute-start | bytes 884744 | tf_op jit(solution)/shard_map/ppermute | solution.py:10
  22.8 0.7 copy-start.2
  25.9 8.5 %collective-permute-start.1 = (bf16[128,1152]{1,0:T(8,128)(2,1)}, bf16[128,1152]{1,0:T(8,128)(2,1)}, u32[]{:S(2)}, u32[]{:S(2)}) collective-permute-start(bf16[128,1152]{1,0:T(8,128)(2,1)} %fusion.1), channel_id=1, source_target_pairs={{8,0},{16,8},{24,16},{0,24},{9,1},{17,9},{25,17},{1,25},{10,2},{18... | collective-permute-start | bytes 884744 | tf_op jit(solution)/shard_map/ppermute | solution.py:10
  45.8 69.2 %reduce-scatter.5.cloned.1.call-start = ((), (), s32[]{:S(2)}) async-start(), calls=%async_computation.2 | async-start | bytes 737280 | tf_op jit(solution)/shard_map/reduce_scatter | solution.py:71
Sparse Core Ops, SparseCore 0:
  46.0 44.6 reduce-scatter.6
  93.0 21.9 reduce-scatter.4
where the time goes:
time: 124 us
  waiting for transfers between devices  78.7 us (63%)
  between operations  15.4 us (12%)
  matrix products  13 us (10%)
  local copies, waits for them, and re-layouts  11.4 us (9%)
  starting transfers between devices  4.9 us (4%)
    unnamed x3, waiting for transfers between devices  44.8 us
    reduce_scatter x1, waiting for transfers between devices, local(): lax.psum_scatter(incomplete_sum, 'blk', scatter_dimension=1, tiled=True)  19.6 us
    ppermute x2, waiting for transfers between devices, shifted(): return lax.ppermute(block, axis, route)  14.3 us
    unnamed x9, local copies, waits for them, and re-layouts  11.4 us
    dot_general x2, matrix products, pair_grad(): lax.dot_general(weights, images, (((0,), (0,)), ((), ())), preferred_elem...  4.82 us
    ppermute x2, starting transfers between devices, shifted(): return lax.ppermute(block, axis, route)  4.82 us
    dot_general x1, matrix products, local(): lax.dot_general(caption_feature_input, row_grad, (((0,), (0,)), ((), ()))...  3.72 us
    dot_general x1, matrix products, local(): lax.dot_general(row_grad, caption_mapping_weights, (((1,), (1,)), ((), ()...  2.79 us
  transfers between devices with their start and end apart: 4, of which 4 were waited for; matrix products, arithmetic and copies ran while one was open for 2% of the time, Pallas kernels for 0%

commit v1 on v0

v1 whole, which is shorter than its diff:
```python
import functools

import jax
import jax.numpy as jnp
from jax import lax
from jax.experimental import pallas as pl
from jax.experimental.pallas import tpu as pltpu
from jax.sharding import PartitionSpec as P

MESH = pl.DeviceIdType.MESH
F32 = jnp.float32
BF16 = jnp.bfloat16


def unit_rows(values):
    radius = jnp.sqrt(jnp.sum(values * values, axis=1, keepdims=True) + 1e-06)
    return values / radius, radius


def edges_of(depth):
    tiles = depth // 128
    first = (tiles + 1) // 2
    return [0, first * 128, depth]


def kernel(
    n_blk,
    n_grp,
    sharp_ref,
    shift_ref,
    pic_hbm,
    feat_hbm,
    head_hbm,
    text_ref,
    out_ref,
    pic,
    feat,
    head,
    pic_next,
    feat_send,
    feat_all,
    rows_all,
    total,
    term_send,
    term_recv,
    local_sem,
    pic_sem,
    feat_sem,
    rows_sem,
    pair_sem,
    term_sem,
):
    blk, grp = lax.axis_index("blk"), lax.axis_index("grp")
    count, depth = feat.shape
    own_rows, own_cols = out_ref.shape
    chips = n_grp // 2
    chip, core = grp // 2, lax.rem(grp, 2)
    sibling = grp + 1 - 2 * core
    edges = edges_of(depth)
    chunks = len(edges) - 1

    loads = [
        pltpu.make_async_copy(feat_hbm, feat, local_sem.at[0]),
        pltpu.make_async_copy(head_hbm, head, local_sem.at[1]),
        pltpu.make_async_copy(pic_hbm, pic, local_sem.at[2]),
    ]
    for load in loads:
        load.start()

    barrier = pltpu.get_barrier_semaphore()
    for d in range(1, n_blk):
        pl.semaphore_signal(
            barrier, inc=1, device_id=(lax.rem(blk + d, n_blk), grp), device_id_type=MESH
        )
    for d in range(1, n_grp):
        pl.semaphore_signal(
            barrier, inc=1, device_id=(blk, lax.rem(grp + d, n_grp)), device_id_type=MESH
        )
    pl.semaphore_wait(barrier, n_blk + n_grp - 2)

    def send(source, target, sems, index, device):
        copy = pltpu.make_async_remote_copy(
            src_ref=source,
            dst_ref=target,
            send_sem=sems.at[(0,) + index],
            recv_sem=sems.at[(1,) + index],
            device_id=device,
            device_id_type=MESH,
        )
        return copy

    pic_copy = send(pic_hbm, pic_next, pic_sem, (0,), (lax.rem(blk + n_blk - 1, n_blk), grp))
    pic_copy.start()

    sharp, shift = sharp_ref[0], shift_ref[0]
    loads[0].wait()
    turned = feat[...].T
    if feat_send.shape[1] != own_rows:
        feat_send[...] = jnp.zeros_like(feat_send)
    for i in range(n_grp):
        feat_send[i, :own_rows, :] = turned[i * own_rows : (i + 1) * own_rows, :]
    here = pl.ds(pl.multiple_of(grp * count, count), count)
    feat_copies = []
    for d in range(1, n_grp):
        other = lax.rem(grp + d, n_grp)
        copy = send(
            feat_send.at[other], feat_all.at[:, here], feat_sem, (d - 1,), (blk, other)
        )
        copy.start()
        feat_copies.append(copy)
    feat_all[:, here] = feat_send[grp]

    loads[1].wait()
    projected = jnp.dot(feat[...], head[...], preferred_element_type=F32)
    unit, radius = unit_rows(projected)
    text_unit = unit.astype(BF16)

    def pair_grad(raw, labels):
        images = unit_rows(raw.astype(F32))[0].astype(BF16)
        logits = (
            sharp
            * lax.dot_general(
                text_unit, images, (((1,), (1,)), ((), ())), preferred_element_type=F32
            )
            + shift
        )
        weights = (jax.nn.sigmoid(logits) - labels).astype(BF16)
        return sharp * jnp.dot(weights, images, preferred_element_type=F32)

    row = lax.broadcasted_iota(jnp.int32, (count, count), 0)
    column = lax.broadcasted_iota(jnp.int32, (count, count), 1)
    loads[2].wait()
    unit_grad = pair_grad(pic[...], jnp.where(row == column, 1.0, 0.0).astype(F32))
    pic_copy.wait_recv()
    unit_grad = unit_grad + pair_grad(pic_next[...], 0.0)
    row_grad = (
        (unit_grad - unit * jnp.sum(unit * unit_grad, axis=1, keepdims=True)) / radius
    ).astype(BF16)
    rows_all[here, :] = row_grad

    pending = []
    far = []
    for j in range(chunks):
        part = pl.ds(edges[j], edges[j + 1] - edges[j])
        block = rows_all.at[here, part]
        far.append([])
        for d in range(1, chips):
            other = 2 * lax.rem(chip + d, chips) + core
            copy = send(block, block, rows_sem, (j, d - 1), (blk, other))
            copy.start()
            far[j].append(copy)
            pending.append(copy)
        copy = send(block, block, pair_sem, (j, 0), (blk, sibling))
        copy.start()
        pending.append(copy)

    text_ref[...] = lax.dot_general(
        row_grad, head[...], (((1,), (1,)), ((), ())), preferred_element_type=F32
    ).astype(BF16)

    for copy in feat_copies:
        copy.wait_recv()

    term_copies = []
    done = 0
    for j in range(chunks):
        part = pl.ds(edges[j], edges[j + 1] - edges[j])
        passed = []
        for d in range(1, chips):
            far[j][d - 1].wait_recv()
            source = 2 * lax.rem(chip + chips - d, chips) + core
            block = rows_all.at[pl.ds(pl.multiple_of(source * count, count), count), part]
            copy = send(block, block, pair_sem, (j, d), (blk, sibling))
            copy.start()
            passed.append(copy)
            pending.append(copy)
        own = rows_all.at[here, part]
        send(own, own, pair_sem, (j, 0), (blk, sibling)).wait_recv()
        for copy in passed:
            copy.wait_recv()
        total[:, part] = jnp.dot(feat_all[...], rows_all[:, part], preferred_element_type=F32)
        while done < n_blk and (done + 1) * own_cols <= edges[j + 1]:
            target = done
            piece = total[:own_rows, target * own_cols : (target + 1) * own_cols]

            @pl.when(blk == target)
            def _():
                out_ref[...] = piece

            @pl.when(blk != target)
            def _():
                slot = lax.rem(target - blk + n_blk, n_blk) - 1
                term_send[target, :own_rows, :] = piece.astype(BF16)
                send(
                    term_send.at[target],
                    term_recv.at[slot],
                    term_sem,
                    (slot,),
                    (target, grp),
                ).start()

            done += 1

    result = out_ref[...]
    for d in range(1, n_blk):
        send(
            term_send.at[0], term_recv.at[d - 1], term_sem, (d - 1,), (blk, grp)
        ).wait_recv()
        result = result + term_recv[d - 1, :own_rows, :].astype(F32)
    out_ref[...] = result

    pic_copy.wait_send()
    for copy in feat_copies + pending:
        copy.wait_send()
    for d in range(1, n_blk):
        send(
            term_send.at[0], term_recv.at[d - 1], term_sem, (d - 1,), (blk, grp)
        ).wait_send()


def local(n_blk, n_grp, pictures, features, head, sharp, shift):
    count, depth = pictures.shape
    own_rows, own_cols = depth // n_grp, depth // n_blk
    padded = -(-own_rows // 16) * 16
    chunks = len(edges_of(depth)) - 1
    sems = pltpu.SemaphoreType.DMA
    return pl.pallas_call(
        functools.partial(kernel, n_blk, n_grp),
        out_shape=(
            jax.ShapeDtypeStruct((count, depth), BF16),
            jax.ShapeDtypeStruct((own_rows, own_cols), F32),
        ),
        in_specs=[pl.BlockSpec(memory_space=pltpu.SMEM)] * 2
        + [pl.BlockSpec(memory_space=pl.ANY)] * 3,
        out_specs=(
            pl.BlockSpec(memory_space=pltpu.VMEM),
            pl.BlockSpec(memory_space=pltpu.VMEM),
        ),
        scratch_shapes=[
            pltpu.VMEM((count, depth), BF16),
            pltpu.VMEM((count, depth), BF16),
            pltpu.VMEM((depth, depth), BF16),
            pltpu.VMEM((count, depth), BF16),
            pltpu.VMEM((n_grp, padded, count), BF16),
            pltpu.VMEM((padded, n_grp * count), BF16),
            pltpu.VMEM((n_grp * count, depth), BF16),
            pltpu.VMEM((padded, depth), F32),
            pltpu.VMEM((n_blk, padded, own_cols), BF16),
            pltpu.VMEM((n_blk - 1, padded, own_cols), BF16),
            sems((3,)),
            sems((2, 1)),
            sems((2, n_grp - 1)),
            sems((2, chunks, n_grp // 2 - 1)),
            sems((2, chunks, n_grp // 2)),
            sems((2, n_blk - 1)),
        ],
        compiler_params=pltpu.CompilerParams(
            collective_id=0, has_side_effects=True, vmem_limit_bytes=40 * 1024 * 1024
        ),
        cost_estimate=pl.CostEstimate(
            flops=8 * count * depth * depth,
            bytes_accessed=2 * depth * (depth + 4 * count),
            transcendentals=2 * count * count,
        ),
    )(sharp, shift, pictures, features, head)


def solution(mesh):
    return jax.shard_map(
        functools.partial(local, mesh.shape["blk"], mesh.shape["grp"]),
        mesh=mesh,
        in_specs=(P(("blk", "grp"), None), P(("blk", "grp"), None), P(), P(), P()),
        out_specs=(P(("blk", "grp"), None), P("grp", "blk")),
        check_vma=False,
    )
```

time: 124 us -> 46.5 us (0.38)
  the two profiles are of different devices: /device:TPU:0 before, /device:TPU:29 now
where the time goes in v1:
time: 46.5 us; the launch traced here: 46.3 us
  Pallas kernels  39.3 us (85%)
  local copies, waits for them, and re-layouts  5.07 us (11%)
  between operations  1.94 us (4%)
    pallas_call x1, Pallas kernels, local(): pl.pallas_call(functools.partial(kernel, n_blk, n_grp), out_shape=(jax.Sh...  39.3 us
    unnamed x8, local copies, waits for them, and re-layouts  5.07 us

profile of v1, /device:TPU:29, one launch (start us, length us, event | category | flops | bytes accessed | tf_op | source)
XLA Modules:
  0.0 46.3 jit_solution(5264272159904513723)
XLA Ops:
  1.9 0.0 copy-start
  1.9 1.7 %copy-done = bf16[1152,1152]{1,0:T(8,128)(2,1)S(1)} copy-done((bf16[1152,1152]{1,0:T(8,128)(2,1)S(1)}, bf16[1152,1152]{1,0:T(8,128)(2,1)}, u32[]{:S(2)}) %copy-start) | copy-done | bytes 2654232
  3.7 0.0 copy-start.1
  3.7 1.0 %copy-done.1 = bf16[128,1152]{1,0:T(8,128)(2,1)S(1)} copy-done((bf16[128,1152]{1,0:T(8,128)(2,1)S(1)}, bf16[128,1152]{1,0:T(8,128)(2,1)}, u32[]{:S(2)}) %copy-start.1) | copy-done | bytes 294936
  4.6 0.0 copy-start.2
  4.6 1.0 %copy-done.2 = bf16[128,1152]{1,0:T(8,128)(2,1)S(1)} copy-done((bf16[128,1152]{1,0:T(8,128)(2,1)S(1)}, bf16[128,1152]{1,0:T(8,128)(2,1)}, u32[]{:S(2)}) %copy-start.2) | copy-done | bytes 294936
  5.6 39.3 %shard_map.68 = (bf16[128,1152]{1,0:T(8,128)(2,1)S(1)}, f32[144,288]{1,0:T(8,128)S(1)}) custom-call(f32[1]{0:T(128)S(6)} %copy.9.sharp_ref, f32[1]{0:T(128)S(6)} %copy.10.shift_ref, bf16[128,1152]{1,0:T(8,128)(2,1)S(1)} %copy-done.1, bf16[128,1152]{1,0:T(8,128)(2,1)S(1)} %copy-done.2, bf16[1152,1152]{1,0:T(8,128)(2,1)S(1)} %copy-done), custom_call_target="tpu_custom_call" | custom-call | flops 1358954496 | bytes 3833856 | tf_op jit(solution)/shard_map/pallas_call | solution.py:227
  44.9 0.7 %copy.11 = bf16[128,1152]{1,0:T(8,128)(2,1)} copy(bf16[128,1152]{1,0:T(8,128)(2,1)S(1)} %get-tuple-element.4) | data formatting | bytes 589824
  45.6 0.7 %copy.12 = f32[144,288]{1,0:T(8,128)} copy(f32[144,288]{1,0:T(8,128)S(1)} %get-tuple-element.5) | data formatting | bytes 331776
Async XLA Ops:
  1.9 1.8 %copy-start = (bf16[1152,1152]{1,0:T(8,128)(2,1)S(1)}, bf16[1152,1152]{1,0:T(8,128)(2,1)}, u32[]{:S(2)}) copy-start(bf16[1152,1152]{1,0:T(8,128)(2,1)} %head_hbm.1) | copy-start | bytes 7962628
  3.7 1.0 %copy-start.1 = (bf16[128,1152]{1,0:T(8,128)(2,1)S(1)}, bf16[128,1152]{1,0:T(8,128)(2,1)}, u32[]{:S(2)}) copy-start(bf16[128,1152]{1,0:T(8,128)(2,1)} %pic_hbm.1) | copy-start | bytes 884740
  4.6 1.0 %copy-start.2 = (bf16[128,1152]{1,0:T(8,128)(2,1)S(1)}, bf16[128,1152]{1,0:T(8,128)(2,1)}, u32[]{:S(2)}) copy-start(bf16[128,1152]{1,0:T(8,128)(2,1)} %feat_hbm.1) | copy-start | bytes 884740

commit v2 on v1

--- a/solution.py
+++ b/solution.py
@@ -17,10 +17,23 @@
     return values / radius, radius
 
 
-def edges_of(depth):
-    tiles = depth // 128
-    first = (tiles + 1) // 2
-    return [0, first * 128, depth]
+def plan(depth, n_blk):
+    width = depth // n_blk
+    order = sorted(range(n_blk), key=lambda i: min(2 * i, 2 * (n_blk - 1 - i) + 1))
+    chunks, pieces, low, high = [], [], 0, depth
+    for piece in order:
+        first = piece * width // 128 * 128
+        last = -(-(piece + 1) * width // 128) * 128
+        start, stop = max(first, low), min(last, high)
+        if start < stop or not chunks:
+            chunks.append((start, stop))
+            pieces.append([])
+            if start == low:
+                low = stop
+            else:
+                high = start
+        pieces[-1].append(piece)
+    return chunks, pieces
 
 
 def kernel(
@@ -56,8 +69,8 @@
     chips = n_grp // 2
     chip, core = grp // 2, lax.rem(grp, 2)
     sibling = grp + 1 - 2 * core
-    edges = edges_of(depth)
-    chunks = len(edges) - 1
+    chunks, pieces = plan(depth, n_blk)
+    square = chips == 4
 
     loads = [
         pltpu.make_async_copy(feat_hbm, feat, local_sem.at[0]),
@@ -139,48 +152,74 @@
     rows_all[here, :] = row_grad
 
     pending = []
-    far = []
-    for j in range(chunks):
-        part = pl.ds(edges[j], edges[j + 1] - edges[j])
-        block = rows_all.at[here, part]
-        far.append([])
-        for d in range(1, chips):
-            other = 2 * lax.rem(chip + d, chips) + core
-            copy = send(block, block, rows_sem, (j, d - 1), (blk, other))
-            copy.start()
-            far[j].append(copy)
-            pending.append(copy)
-        copy = send(block, block, pair_sem, (j, 0), (blk, sibling))
+
+    def rows_of(other_chip, other_core, part, start=0, size=count):
+        first = (2 * other_chip + other_core) * count + start
+        return rows_all.at[pl.ds(pl.multiple_of(first, 16), size), part]
+
+    def go(block, sems, index, device):
+        copy = send(block, block, sems, index, device)
         copy.start()
         pending.append(copy)
-
-    text_ref[...] = lax.dot_general(
-        row_grad, head[...], (((1,), (1,)), ((), ())), preferred_element_type=F32
-    ).astype(BF16)
-
-    for copy in feat_copies:
-        copy.wait_recv()
-
-    term_copies = []
-    done = 0
-    for j in range(chunks):
-        part = pl.ds(edges[j], edges[j + 1] - edges[j])
-        passed = []
-        for d in range(1, chips):
-            far[j][d - 1].wait_recv()
-            source = 2 * lax.rem(chip + chips - d, chips) + core
-            block = rows_all.at[pl.ds(pl.multiple_of(source * count, count), count), part]
-            copy = send(block, block, pair_sem, (j, d), (blk, sibling))
-            copy.start()
-            passed.append(copy)
-            pending.append(copy)
-        own = rows_all.at[here, part]
-        send(own, own, pair_sem, (j, 0), (blk, sibling)).wait_recv()
-        for copy in passed:
-            copy.wait_recv()
+        return copy
+
+    beside = chip + 1 - 2 * lax.rem(chip, 2)
+    above = lax.rem(chip + 2, 4)
+    across = 3 - chip
+    half = count // 2
+    parts = [pl.ds(start, stop - start) for start, stop in chunks]
+    far = []
+
+    def first_sends(j):
+        block = rows_of(chip, core, parts[j])
+        if square:
+            far.append(
+                [
+                    go(block, rows_sem, (j, 0), (blk, 2 * beside + core)),
+                    go(block, rows_sem, (j, 1), (blk, 2 * above + core)),
+                ]
+            )
+        else:
+            far.append(
+                [
+                    go(block, rows_sem, (j, d - 1), (blk, 2 * lax.rem(chip + d, chips) + core))
+                    for d in range(1, chips)
+                ]
+            )
+        go(block, pair_sem, (j, 0), (blk, sibling))
+
+    def relay(j):
+        part = parts[j]
+        if square:
+            far[j][0].wait_recv()
+            there = (blk, 2 * above + core)
+            far[j].append(go(rows_of(beside, core, part, 0, half), rows_sem, (j, 2), there))
+            go(rows_of(beside, core, part), pair_sem, (j, 1), (blk, sibling))
+            far[j][1].wait_recv()
+            there = (blk, 2 * beside + core)
+            far[j].append(go(rows_of(above, core, part, half, half), rows_sem, (j, 3), there))
+            go(rows_of(above, core, part), pair_sem, (j, 2), (blk, sibling))
+
+    def finish(j):
+        part = parts[j]
+        blocks = [rows_of(chip, core, part)]
+        if square:
+            blocks += [rows_of(beside, core, part), rows_of(above, core, part)]
+            for i in range(2):
+                far[j][2 + i].wait_recv()
+                block = rows_of(across, core, part, i * half, half)
+                go(block, pair_sem, (j, 3 + i), (blk, sibling))
+                blocks.append(block)
+        else:
+            for d in range(1, chips):
+                far[j][d - 1].wait_recv()
+                block = rows_of(lax.rem(chip + chips - d, chips), core, part)
+                go(block, pair_sem, (j, d), (blk, sibling))
+                blocks.append(block)
+        for i, block in enumerate(blocks):
+            send(block, block, pair_sem, (j, i), (blk, sibling)).wait_recv()
         total[:, part] = jnp.dot(feat_all[...], rows_all[:, part], preferred_element_type=F32)
-        while done < n_blk and (done + 1) * own_cols <= edges[j + 1]:
-            target = done
+        for target in pieces[j]:
             piece = total[:own_rows, target * own_cols : (target + 1) * own_cols]
 
             @pl.when(blk == target)
@@ -199,7 +238,24 @@
                     (target, grp),
                 ).start()
 
-            done += 1
+    ahead = min(2, len(chunks))
+    for j in range(ahead):
+        first_sends(j)
+
+    text_ref[...] = lax.dot_general(
+        row_grad, head[...], (((1,), (1,)), ((), ())), preferred_element_type=F32
+    ).astype(BF16)
+
+    for copy in feat_copies:
+        copy.wait_recv()
+
+    for j in range(len(chunks)):
+        relay(j)
+        if j + ahead < len(chunks):
+            first_sends(j + ahead)
+        if j:
+            finish(j - 1)
+    finish(len(chunks) - 1)
 
     result = out_ref[...]
     for d in range(1, n_blk):
@@ -222,7 +278,7 @@
     count, depth = pictures.shape
     own_rows, own_cols = depth // n_grp, depth // n_blk
     padded = -(-own_rows // 16) * 16
-    chunks = len(edges_of(depth)) - 1
+    chunks = len(plan(depth, n_blk)[0])
     sems = pltpu.SemaphoreType.DMA
     return pl.pallas_call(
         functools.partial(kernel, n_blk, n_grp),
@@ -231,7 +287,7 @@
             jax.ShapeDtypeStruct((own_rows, own_cols), F32),
         ),
         in_specs=[pl.BlockSpec(memory_space=pltpu.SMEM)] * 2
-        + [pl.BlockSpec(memory_space=pl.ANY)] * 3,
+        + [pl.BlockSpec(memory_space=pltpu.HBM)] * 3,
         out_specs=(
             pl.BlockSpec(memory_space=pltpu.VMEM),
             pl.BlockSpec(memory_space=pltpu.VMEM),
@@ -250,12 +306,12 @@
             sems((3,)),
             sems((2, 1)),
             sems((2, n_grp - 1)),
-            sems((2, chunks, n_grp // 2 - 1)),
-            sems((2, chunks, n_grp // 2)),
+            sems((2, chunks, max(4, n_grp // 2 - 1))),
+            sems((2, chunks, max(5, n_grp // 2))),
             sems((2, n_blk - 1)),
         ],
         compiler_params=pltpu.CompilerParams(
-            collective_id=0, has_side_effects=True, vmem_limit_bytes=40 * 1024 * 1024
+            collective_id=0, has_side_effects=True, vmem_limit_bytes=60 * 1024 * 1024
         ),
         cost_estimate=pl.CostEstimate(
             flops=8 * count * depth * depth,

time: 46.5 us -> 42 us (0.903)
  the two profiles are of different devices: /device:TPU:29 before, /device:TPU:17 now
where the time goes in v2:
time: 42 us; the launch traced here: 41.8 us
  Pallas kernels  36.5 us (87%)
  local copies, waits for them, and re-layouts  3.33 us (8%)
  between operations  1.93 us (5%)
    pallas_call x1, Pallas kernels, local(): pl.pallas_call(functools.partial(kernel, n_blk, n_grp), out_shape=(jax.Sh...  36.5 us
    unnamed x2, local copies, waits for them, and re-layouts  3.33 us

profile of v2, /device:TPU:17, one launch (start us, length us, event | category | flops | bytes accessed | tf_op | source)
XLA Modules:
  0.0 41.8 jit_solution(13743246791121313614)
XLA Ops:
  1.9 36.5 %shard_map.68 = (bf16[128,1152]{1,0:T(8,128)(2,1)}, f32[144,288]{1,0:T(8,128)}) custom-call(f32[1]{0:T(128)S(6)} %copy.9.sharp_ref, f32[1]{0:T(128)S(6)} %copy.10.shift_ref, bf16[128,1152]{1,0:T(8,128)(2,1)} %pic_hbm.1, bf16[128,1152]{1,0:T(8,128)(2,1)} %feat_hbm.1, bf16[1152,1152]{1,0:T(8,128)(2,1)} %head_hbm.1), custom_call_target="tpu_custom_call" | custom-call | flops 1358954496 | bytes 3833856 | tf_op jit(solution)/shard_map/pallas_call | solution.py:283
  38.5 1.7 %copy.11 = bf16[128,1152]{1,0:T(8,128)(2,1)} copy(bf16[128,1152]{1,0:T(8,128)(2,1)} %get-tuple-element.4) | data formatting | bytes 589824
  40.2 1.6 %copy.12 = f32[144,288]{1,0:T(8,128)} copy(f32[144,288]{1,0:T(8,128)} %get-tuple-element.5) | data formatting | bytes 331776
